TPU v7x, 256 devices: a whole 4x4x8 slice. The times are simulated.
256 devices in a mesh: ctx: 64 (over x_lo, y, z), head: 4 (over x_hi, core).
Axes of the slice: x: 4 (x_hi: 2, x_lo: 2; x = x_hi * 2 + x_lo), y: 4, z: 8, core: 2. Of those that a mesh axis runs over, the one named last changes fastest.
Arguments:
- tokens: bfloat16 [16384, 4096], P(('ctx', 'head')), may hold values from -24 to 24
- w_query: bfloat16 [4096, 4096], P(None, 'head'), may hold values from -0.09375 to 0.09375
- w_key: bfloat16 [4096, 512], P(None, 'head'), may hold values from -0.09375 to 0.09375
- w_value: bfloat16 [4096, 512], P(None, 'head'), may hold values from -0.09375 to 0.09375
- block_order: int32 [128], replicated, may hold values from 0 to 127, each once
Outputs:
- attended: bfloat16 [16384, 4096], P('ctx', 'head')
All inputs are finite; a program needn't handle non-finite values.
Results may differ from a plain program's by a relative error of at most 0.0075.
The roundings to bfloat16 on the way count: a program that leaves them out, or rounds other values in their place, can miss the bound.
Values may be sent and summed in bfloat16 or wider, within the bound.
A program may use at most 128 MiB of HBM per device.

v0:
```python
import math

import jax
import jax.numpy as jnp
import numpy as np
from jax import lax
from jax.sharding import PartitionSpec as P

HD = 128
BLK = 128


def rotary_tables(count):
    half = HD // 2
    freqs = 500000.0 ** (-(np.arange(half) * 2.0) / HD)
    angles = (np.arange(count) * 1.0)[:, None] * freqs[None, :]
    return (jnp.asarray(np.cos(angles), jnp.float32), jnp.asarray(np.sin(angles), jnp.float32))


def rotate(values, cosine, sine, heads):
    count = values.shape[0]
    half = HD // 2
    split = values.reshape(count, heads, HD)
    first = split[:, :, :half]
    second = split[:, :, half:]
    cos_part = cosine[:, None, :]
    sin_part = sine[:, None, :]
    joined = jnp.concatenate(
        [first * cos_part - second * sin_part, second * cos_part + first * sin_part], 2
    )
    return joined.reshape(count, heads * HD)


def three_products(rows_in, w_query, w_key, w_value):
    return jnp.concatenate(
        [
            jnp.dot(rows_in, w_query, preferred_element_type=jnp.float32),
            jnp.dot(rows_in, w_key, preferred_element_type=jnp.float32),
            jnp.dot(rows_in, w_value, preferred_element_type=jnp.float32),
        ],
        1,
    )


def per_device(tokens, w_query, w_key, w_value, block_order):
    ctx_count = lax.axis_size("ctx")
    ctx_index = lax.axis_index("ctx")
    q_width = w_query.shape[1]
    kv_width = w_key.shape[1]
    q_heads = q_width // HD
    kv_heads = kv_width // HD
    group = q_heads // kv_heads
    local_rows = tokens.shape[0] * lax.axis_size("head")
    sub_count = local_rows // BLK
    scale = 1.0 / math.sqrt(HD)
    whole = lax.all_gather(tokens, "head", axis=0, tiled=True)
    mixed = three_products(whole, w_query, w_key, w_value)
    own_blocks = lax.dynamic_slice_in_dim(block_order, ctx_index * sub_count, sub_count, 0)
    offsets = jnp.arange(BLK, dtype=jnp.int32)
    own_pos = (own_blocks[:, None] * BLK + offsets[None, :]).reshape(-1)
    cos_table, sin_table = rotary_tables(local_rows * ctx_count)
    cosine = jnp.take(cos_table, own_pos, axis=0)
    sine = jnp.take(sin_table, own_pos, axis=0)
    query = rotate(mixed[:, :q_width], cosine, sine, q_heads).astype(jnp.bfloat16)
    key = rotate(mixed[:, q_width : q_width + kv_width], cosine, sine, kv_heads).astype(
        jnp.bfloat16
    )
    value = mixed[:, q_width + kv_width :].astype(jnp.bfloat16)
    query_split = query.reshape(local_rows, kv_heads, group, HD)
    initial = tuple(
        (
            (
                jnp.full((kv_heads, group, BLK), -1e30, jnp.float32),
                jnp.zeros((kv_heads, group, BLK), jnp.float32),
                jnp.zeros((kv_heads, group, BLK, HD), jnp.float32),
            )
            for index in range(sub_count)
        )
    )
    key_piece = lax.all_gather(key, "ctx", axis=0, tiled=True)
    value_piece = lax.all_gather(value, "ctx", axis=0, tiled=True)
    size = key_piece.shape[0]
    tile = math.gcd(size, BLK)

    def one_tile(step, state):
        first_row = step * tile
        key_tile = lax.dynamic_slice_in_dim(key_piece, step * tile, tile, 0).reshape(
            tile, kv_heads, HD
        )
        value_tile = lax.dynamic_slice_in_dim(value_piece, step * tile, tile, 0).reshape(
            tile, kv_heads, HD
        )
        base_block = lax.dynamic_slice_in_dim(block_order, first_row // BLK, 1, 0)[0]
        key_pos = base_block * BLK + first_row % BLK + jnp.arange(tile, dtype=jnp.int32)
        lowest = base_block * BLK + first_row % BLK
        updated = []
        for index in range(sub_count):
            query_rows = query_split[index * BLK : (index + 1) * BLK]
            query_pos = own_pos[index * BLK : (index + 1) * BLK]

            def attend(entry, query_rows=query_rows, query_pos=query_pos):
                running_max, running_total, running_acc = entry
                scores = (
                    jnp.einsum(
                        "qkgd,skd->kgqs", query_rows, key_tile, preferred_element_type=jnp.float32
                    )
                    * scale
                )
                keep = (key_pos[None, :] <= query_pos[:, None])[None, None]
                scores = jnp.where(keep, scores, -1e30)
                new_max = jnp.maximum(running_max, jnp.max(scores, axis=3))
                expo = jnp.where(keep, jnp.exp(scores - new_max[..., None]), 0.0)
                factor = jnp.exp(running_max - new_max)
                new_total = running_total * factor + jnp.sum(expo, axis=3)
                product = jnp.einsum(
                    "kgqs,skd->kgqd",
                    expo.astype(jnp.bfloat16),
                    value_tile,
                    preferred_element_type=jnp.float32,
                )
                return (new_max, new_total, running_acc * factor[..., None] + product)

            def unchanged(entry):
                return entry

            updated.append(
                lax.cond(
                    lowest <= own_blocks[index] * BLK + BLK - 1, attend, unchanged, state[index]
                )
            )
        return tuple(updated)

    final = lax.fori_loop(0, size // tile, one_tile, initial)
    outputs = []
    for index in range(sub_count):
        running_max, running_total, running_acc = final[index]
        normed = running_acc / running_total[..., None]
        outputs.append(jnp.transpose(normed, (2, 0, 1, 3)).reshape(BLK, q_width))
    return jnp.concatenate(outputs, 0).astype(jnp.bfloat16)


def solution(mesh):
    return jax.shard_map(
        per_device,
        mesh=mesh,
        in_specs=(P(("ctx", "head"), None), P(None, "head"), P(None, "head"), P(None, "head"), P()),
        out_specs=P("ctx", "head"),
        check_vma=False,
    )
```

profile of v0, /device:TPU:250, one launch (start us, length us, event | category | flops | bytes accessed | tf_op | source)
XLA Modules:
  0.0 1220.2 jit_solution(5950937866571757978)
XLA Ops:
  8.1 4.1 gather_fusion
  12.3 4.1 gather_fusion.1
  16.5 21.1 %all-gather.5.cloned.1.call-done = bf16[256,4096]{1,0:T(8,128)(2,1)} async-done(((bf16[64,4096]{1,0:T(8,128)(2,1)}), bf16[256,4096]{1,0:T(8,128)(2,1)}) %all-gather.5.cloned.1.call-update) | async-done | bytes 2097168 | tf_op jit(solution)/shard_map/all_gather | solution.py:56
  37.6 2.4 convolution_bitcast_fusion.3
  40.8 2.9 convolution_convert_fusion
  45.8 6.3 convolution_bitcast_fusion.2
  53.4 229.4 %all-gather.9.cloned.1.call-done = bf16[16384,1,128]{0,2,1:T(8,128)(2,1)} async-done(((bf16[256,1,128]{0,2,1:T(8,128)(2,1)}), bf16[16384,1,128]{0,2,1:T(8,128)(2,1)}) %all-gather.9.cloned.1.call-update) | async-done | bytes 4194320 | tf_op jit(solution)/shard_map/all_gather | solution.py:80
  282.8 303.1 %all-gather.7.cloned.1.call-done = bf16[16384,128]{1,0:T(8,128)(2,1)} async-done(((bf16[256,128]{1,0:T(8,128)(2,1)}), bf16[16384,128]{1,0:T(8,128)(2,1)}) %all-gather.7.cloned.1.call-update) | async-done | bytes 4194320 | tf_op jit(solution)/shard_map/all_gather | solution.py:81
  586.0 626.0 %while.27 = (s32[]{:T(128)}, f32[1,8,128]{2,1,0:T(8,128)S(1)}, f32[1,8,128]{2,1,0:T(8,128)S(1)}, f32[1,8,128,128]{3,2,1,0:T(8,128)S(1)}, f32[1,8,128]{2,1,0:T(8,...) while((s32[]{:T(128)}, f32[1,8,128]{2,1,0:T(8,128)S(1)}, ...), condition=%wide.region_9.11_spmd.clone, body=%wide.region_0.10_spmd.clone.sunk | while | flops 137140640 | bytes 6363403 | solution.py:133
  590.0 1.0 conditional.6
  597.9 1.0 conditional.6
  602.9 1.0 conditional.6
  607.9 1.0 conditional.6
  612.8 1.0 conditional.6
  617.8 1.0 conditional.6
  622.7 1.0 conditional.6
  627.7 1.0 conditional.6
  632.7 1.0 conditional.6
  637.6 1.0 conditional.6
  642.6 1.0 conditional.6
  647.5 1.0 conditional.6
  652.5 1.0 conditional.6
  657.5 1.0 conditional.6
  662.4 1.0 conditional.6
  667.4 1.0 conditional.6
  672.3 1.0 conditional.6
  677.3 1.0 conditional.6
  685.3 1.0 conditional.6
  690.2 1.0 conditional.6
  695.2 1.0 conditional.6
  700.1 1.0 conditional.6
  705.1 1.0 conditional.6
  715.0 1.0 conditional.6
  724.9 1.0 conditional.6
  734.9 1.0 conditional.6
  744.8 1.0 conditional.6
  754.7 1.0 conditional.6
  764.6 1.0 conditional.6
  774.5 1.0 conditional.6
  784.5 1.0 conditional.6
  794.4 1.0 conditional.6
  804.3 1.0 conditional.6
  814.2 1.0 conditional.6
  824.1 1.0 conditional.6
  834.1 1.0 conditional.6
  844.0 1.0 conditional.6
  853.9 1.0 conditional.6
  863.8 1.0 conditional.6
  (3000 shorter events, 717.9 us)
Async XLA Ops:
  6.5 31.1 %copy-start = (bf16[4096,128]{1,0:T(8,128)(2,1)S(1)}, bf16[4096,128]{1,0:T(8,128)(2,1)}, u32[]{:S(2)}) copy-start(bf16[4096,128]{1,0:T(8,128)(2,1)} %param.17) | copy-start | bytes 3145732
  6.5 34.3 %copy-start.1 = (bf16[4096,128]{1,0:T(8,128)(2,1)S(1)}, bf16[4096,128]{1,0:T(8,128)(2,1)}, u32[]{:S(2)}) copy-start(bf16[4096,128]{1,0:T(8,128)(2,1)} %param.18) | copy-start | bytes 3145732
  6.5 31.1 %all-gather.5.cloned.1.call-start = ((), (), s32[]{:S(2)}) async-start(), calls=%async_computation | async-start | bytes 2621440 | tf_op jit(solution)/shard_map/all_gather | solution.py:56
  7.3 275.5 %all-gather.9.cloned.1.call-start = ((), (), s32[]{:S(2)}) async-start(), calls=%async_computation.2 | async-start | bytes 4259840 | tf_op jit(solution)/shard_map/all_gather | solution.py:80
  40.7 545.1 %all-gather.7.cloned.1.call-start = ((), (), s32[]{:S(2)}) async-start(), calls=%async_computation.1 | async-start | bytes 4259840 | tf_op jit(solution)/shard_map/all_gather | solution.py:81
  52.3 533.7 %copy-start.2 = (s32[128]{0:T(128)S(1)}, s32[128]{0:T(128)}, u32[]{:S(2)}) copy-start(s32[128]{0:T(128)} %param.19) | copy-start | bytes 1540
Sparse Core Ops, SparseCore 0:
  9.2 28.3 all-gather.4
  40.9 241.8 all-gather.8
  284.5 301.2 all-gather.6
where the time goes:
time: 1240 us; the launch traced here: 1220 us
  waiting for transfers between devices  554 us (45%)
  local copies, waits for them, and re-layouts  298 us (24%)
  matrix products  178 us (14%)
  loops' own time  111 us (9%)
  other arithmetic  64.1 us (5%)
  between operations  14.5 us (1%)
    all_gather x1, waiting for transfers between devices, per_device(): value_piece = lax.all_gather(value, 'ctx', axis=0, tiled=True)  303 us
    all_gather x1, waiting for transfers between devices, per_device(): key_piece = lax.all_gather(key, 'ctx', axis=0, tiled=True)  229 us
    dynamic_slice x256, local copies, waits for them, and re-layouts, one_tile(): lax.dynamic_slice_in_dim(key_piece, step * tile, tile, 0)  112 us
    dot_general x247, matrix products, attend(): jnp.einsum('kgqs,skd->kgqd', expo.astype(jnp.bfloat16), value_tile, prefe...  107 us
    reshape x128, local copies, waits for them, and re-layouts, one_tile(): lax.dynamic_slice_in_dim(value_piece, step * tile, tile, 0)  98.8 us
    another operation x1, loops' own time, per_device(): final = lax.fori_loop(0, size // tile, one_tile, initial)  96.4 us
    dynamic_slice x128, local copies, waits for them, and re-layouts, one_tile(): lax.dynamic_slice_in_dim(block_order, first_row // BLK, 1, 0)[0]  75.1 us
    dot_general x247, matrix products, attend(): jnp.einsum('qkgd,skd->kgqs', query_rows, key_tile, preferred_element_type...  59.3 us
  transfers between devices with their start and end apart: 3, of which 3 were waited for; matrix products, arithmetic and copies ran while one was open for 2% of the time, Pallas kernels for 0%

commit v1 on v0

v1 whole, which is shorter than its diff:
```python
import math

import jax
import jax.numpy as jnp
import numpy as np
from jax import lax
from jax.experimental import pallas as pl
from jax.experimental.pallas import tpu as pltpu
from jax.sharding import PartitionSpec as P

HD = 128
BLK = 128
NX, NY, NZ = 2, 4, 8
STEPS = 16
PAIRS = 4
TILE = 256
LOW = -1e30
FACTOR = math.log2(math.e) / math.sqrt(HD)
CONTRACT_LAST = (((1,), (1,)), ((), ()))
MOVES = {"x": (1, 0, 0), "y+": (0, 1, 0), "y-": (0, -1, 0), "z+": (0, 0, 1), "z-": (0, 0, -1)}


def moved(item, way):
    kind, x, y, z = item
    dx, dy, dz = MOVES[way]
    return (kind, (x + dx) % NX, (y + dy) % NY, (z + dz) % NZ)


def all_messages():
    out = [("x", (("E", 0, 0, 0),)), ("x", (("L", 0, 0, 0),))]

    def pair(kind, y, z):
        return ((kind, 0, y, z), (kind, 1, y, z))

    for x in range(NX):
        out += [("z+", (("E", x, 0, 0),)), ("z-", (("E", x, 0, 0),))]
    out += [("z+", pair("E", 0, 1)), ("z+", pair("E", 0, 2))]
    out += [("z-", pair("E", 0, 7)), ("z-", pair("E", 0, 6))]
    out += [("z+", (("E", 0, 0, 3),)), ("z-", (("E", 1, 0, 5),))]
    for z in range(NZ):
        out += [("y+", pair("E", 0, z)), ("y-", pair("E", 0, z))]
        out += [("y+", pair("E", 1, z)) if z % 2 == 0 else ("y-", pair("E", 3, z))]
    out += [("y+", pair("L", 0, 0)), ("y-", pair("L", 0, 0))]
    out += [("y+", (("L", 0, 1, 0),)), ("y-", (("L", 1, 3, 0),))]
    for y in range(NY):
        for z in (0, 1, 2):
            out += [("z+", pair("L", y, z)), ("z-", pair("L", y, -z % NZ))]
        out += [("z+", pair("L", y, 3)) if y % 2 == 0 else ("z-", pair("L", y, 5))]
    return out


def plan():
    messages = all_messages()
    block_us, latency = 1.42, 2.4
    segments = [("qE", 0.8)] * 4 + [("kvL", 1.0)] + [("qL", 0.8)] * 4 + [("own", 0.6)]
    segments += [("step", 3.0)] * STEPS
    have = {("E", 0, 0, 0)}
    free = {way: 0.0 for way in MOVES}
    arrival, unsent, arrived, used = {}, list(range(len(messages))), set(), set()
    now = 4.0
    actions, order = [], []

    def send_ready(acts):
        for m in list(unsent):
            way, items = messages[m]
            if all(item in have for item in items):
                unsent.remove(m)
                free[way] = max(now, free[way]) + block_us * len(items)
                arrival[m] = free[way] + latency
                acts.append(("send", m))

    def take(m, acts):
        nonlocal now
        acts.append(("wait", m))
        now = max(now, arrival[m])
        arrived.add(m)
        have.update(moved(item, messages[m][0]) for item in messages[m][1])
        send_ready(acts)

    def pending():
        return sorted((arrival[m], m) for m in arrival if m not in arrived)

    def ready_pairs():
        return [
            (k, y, z)
            for k, x, y, z in sorted(have, key=lambda item: when.get(item, 0.0))
            if x == 0 and (k, 1, y, z) in have and (k, y, z) not in used
        ]

    when = {}
    for what, length in segments:
        acts = []
        if what == "kvL":
            now = max(now, 13.0)
        send_ready(acts)
        while True:
            soon = [(t, m) for t, m in pending() if t <= now]
            if not soon:
                break
            take(soon[0][1], acts)
        if what == "step":
            while len(ready_pairs()) < PAIRS:
                take(pending()[0][1], acts)
            chosen = ready_pairs()[:PAIRS]
            used.update(chosen)
            order.append(chosen)
        actions.append((what, acts))
        now += length
        if what == "kvL":
            have.add(("L", 0, 0, 0))
    assert len(arrived) == len(messages)
    place = {
        (k, x, y, z): (step, p * NX + x)
        for step, chosen in enumerate(order)
        for p, (k, y, z) in enumerate(chosen)
        for x in range(NX)
    }
    assert len(place) == 2 * NX * NY * NZ
    return messages, actions, place, now


MESSAGES, ACTIONS, PLACE, ESTIMATE = plan()


def kernel(
    tok_in, wq_in, wk_in, wv_in, table, aug, out,
    tok, wq, wkv, query, kv, largest, acc,
    send, recv, tok_sem, relay_sem, local,
):
    ctx, head = lax.axis_index("ctx"), lax.axis_index("head")
    x, y, z = ctx // 32, (ctx // 8) % 4, ctx % 8
    core = head % 2

    def device(x, y, z):
        return ((x * 4 + y) * 8 + z, head)

    near = {
        "x": device(1 - x, y, z),
        "y+": device(x, (y + 1) % 4, z),
        "y-": device(x, (y + 3) % 4, z),
        "z+": device(x, y, (z + 1) % 8),
        "z-": device(x, y, (z + 7) % 8),
    }
    beside = (ctx, head + 1 - 2 * core)
    across = (ctx, (head + 2) % 4)

    copies = [
        pltpu.make_async_copy(wk_in, wkv.at[:, 0:HD], local.at[0]),
        pltpu.make_async_copy(wv_in, wkv.at[:, HD : 2 * HD], local.at[1]),
    ]
    mine = pl.ds(pl.multiple_of(core * 64, 64), 64)
    own_tokens = pltpu.make_async_copy(tok_in, tok.at[0, mine], local.at[2])
    own_tokens.start()
    for copy in copies:
        copy.start()
    wide = []
    for j in range(4):
        columns = pl.ds(j * TILE, TILE)
        wide.append(pltpu.make_async_copy(wq_in.at[:, columns], wq.at[:, columns], local.at[3 + j]))
        wide[-1].start()

    barrier = pltpu.get_barrier_semaphore()
    peers = list(near.values()) + [beside, across]
    for peer in peers:
        pl.semaphore_signal(barrier, inc=1, device_id=peer, device_id_type=pl.DeviceIdType.MESH)
    pl.semaphore_wait(barrier, len(peers))

    def remote(src, dst, s, r, to):
        return pltpu.make_async_remote_copy(
            src_ref=src, dst_ref=dst, send_sem=s, recv_sem=r, device_id=to,
            device_id_type=pl.DeviceIdType.MESH,
        )

    to_beside = remote(tok_in, tok.at[0, mine], tok_sem.at[0], tok_sem.at[1], beside)
    to_beside.start()
    to_across, relays = [], []
    for j in range(4):
        rows = pl.ds(pl.multiple_of(core * 64 + j * 16, 16), 16)
        to_across.append(
            remote(tok_in.at[pl.ds(j * 16, 16)], tok.at[1, rows], tok_sem.at[2 + j], tok_sem.at[6 + j], across)
        )
        to_across[-1].start()
        relays.append(
            remote(tok.at[1, rows], tok.at[1, rows], relay_sem.at[j], relay_sem.at[4 + j], beside)
        )

    def slot(items):
        step, p = PLACE[items[0]]
        return kv.at[step, :, pl.ds(p * BLK, BLK * len(items))]

    def message(m):
        way, items = MESSAGES[m]
        landing = [moved(item, way) for item in items]
        landing.sort(key=lambda item: PLACE[item])
        taking = sorted(items, key=lambda item: PLACE[item])
        assert len(items) == 1 or way != "x"
        return remote(slot(taking), slot(landing), send.at[m], recv.at[m], near[way])

    def communicate(acts):
        for what, m in acts:
            if what == "send":
                message(m).start()
            else:
                message(m).wait_recv()

    def rotated(values, part):
        pieces = table[part]
        swapped = pltpu.roll(pieces, HD // 2, 1)
        first = lax.broadcasted_iota(jnp.int32, pieces.shape, 1) < HD // 2
        cosine = jnp.where(first, pieces, swapped)
        sine = jnp.where(first, -swapped, pieces)
        return (values * cosine + pltpu.roll(values, HD // 2, 1) * sine).astype(jnp.bfloat16)

    def project_kv(part, kind):
        both = jnp.dot(tok[part], wkv[...], preferred_element_type=jnp.float32)
        step, p = PLACE[(kind, 0, 0, 0)]
        rows = pl.ds(p * BLK, BLK)
        kv[step, 0, rows] = rotated(both[:, :HD], part)
        kv[step, 1, rows] = both[:, HD:].astype(jnp.bfloat16)

    def project_q(part, j):
        both = jnp.dot(tok[part], wq[:, j * TILE : (j + 1) * TILE], preferred_element_type=jnp.float32)
        for h in range(2):
            rows = pl.ds(part * 1024 + (2 * j + h) * BLK, BLK)
            query[rows] = rotated(both[:, h * HD : (h + 1) * HD], part)

    lane = lax.broadcasted_iota(jnp.int32, (TILE, HD), 1)
    marks = [jnp.where(lane == part, 1.0, 0.0).astype(jnp.bfloat16) for part in range(2)]

    def own_blocks():
        ones = jnp.ones((BLK, HD), jnp.bfloat16)
        row = lax.broadcasted_iota(jnp.int32, (TILE, BLK), 0) % BLK
        keep = lax.broadcasted_iota(jnp.int32, (TILE, BLK), 1) <= row
        for part, kind in enumerate("EL"):
            step, p = PLACE[(kind, 0, 0, 0)]
            keys = kv[step, 0, pl.ds(p * BLK, BLK)]
            values = jnp.concatenate([kv[step, 1, pl.ds(p * BLK, BLK)], ones], 1)
            for t in range(4):
                rows = pl.ds(part * 1024 + t * TILE, TILE)
                scores = lax.dot_general(query[rows], keys, CONTRACT_LAST, preferred_element_type=jnp.float32)
                scores = jnp.where(keep, scores, LOW)
                top = jnp.broadcast_to(jnp.max(scores, axis=1, keepdims=True), (TILE, HD))
                expo = jnp.exp2((scores - top) * FACTOR).astype(jnp.bfloat16)
                largest[rows] = top
                acc[rows] = jnp.dot(expo, values, preferred_element_type=jnp.float32)

    def attend(step):
        masks = [
            jnp.concatenate([aug[step, b]] * (BLK // 16), 0) for b in range(2 * PAIRS)
        ]
        keys = jnp.concatenate([kv[step, 0], jnp.concatenate(masks, 0)], 1)
        values = jnp.concatenate([kv[step, 1], jnp.ones((1024, HD), jnp.bfloat16)], 1)
        for t in range(8):
            rows = pl.ds(t * TILE, TILE)
            wide_query = jnp.concatenate([query[rows], marks[t // 4]], 1)
            scores = lax.dot_general(wide_query, keys, CONTRACT_LAST, preferred_element_type=jnp.float32)
            before = largest[rows]
            after = jnp.maximum(before, jnp.max(scores, axis=1, keepdims=True))
            largest[rows] = after
            expo = jnp.concatenate(
                [jnp.exp2((scores[:, b * HD : (b + 1) * HD] - after) * FACTOR).astype(jnp.bfloat16) for b in range(8)], 1
            )
            shrink = jnp.exp2((before - after) * FACTOR)
            product = jnp.dot(expo, values, preferred_element_type=jnp.float32)
            acc[rows] = acc[rows] * jnp.concatenate([shrink, shrink], 1) + product

    own_tokens.wait()
    to_beside.wait_recv()
    for copy in copies:
        copy.wait()
    project_kv(0, "E")
    step_acts = []
    j = {"qE": 0, "qL": 0}
    for what, acts in ACTIONS:
        if what == "step":
            step_acts.append(acts)
            continue
        communicate(acts)
        if what == "qE":
            wide[j[what]].wait()
            project_q(0, j[what])
            j[what] += 1
        elif what == "kvL":
            for k in range(4):
                to_across[k].wait_recv()
                relays[k].start()
            for k in range(4):
                relays[k].wait_recv()
            project_kv(1, "L")
        elif what == "qL":
            project_q(1, j[what])
            j[what] += 1
        else:
            own_blocks()

    def one_step(step, carry):
        for s, acts in enumerate(step_acts):
            if acts:

                @pl.when(step == s)
                def _(acts=acts):
                    communicate(acts)

        attend(step)
        return carry

    lax.fori_loop(0, STEPS, one_step, 0)

    early = head // 2
    for part in range(2):
        block = pl.ds(pl.multiple_of((early if part == 0 else 1 - early) * BLK, BLK), BLK)
        for h in range(8):
            rows = pl.ds(part * 1024 + h * BLK, BLK)
            total = acc[rows]
            out[block, h * HD : (h + 1) * HD] = (total[:, :HD] / total[:, HD:]).astype(jnp.bfloat16)

    for m in range(len(MESSAGES)):
        message(m).wait_send()
    to_beside.wait_send()
    for k in range(4):
        to_across[k].wait_send()
        relays[k].wait_send()


def rotary_table(count):
    half = HD // 2
    freqs = 500000.0 ** (-(np.arange(half) * 2.0) / HD)
    angles = (np.arange(count) * 1.0)[:, None] * freqs[None, :]
    joined = np.concatenate([np.cos(angles), np.sin(angles)], 1)
    return jnp.asarray(joined.reshape(count // BLK, BLK, HD), jnp.float32)


def origins():
    inverse = {where: item for item, where in PLACE.items()}
    rows = []
    for step in range(STEPS):
        for b in range(2 * PAIRS):
            kind, x, y, z = inverse[(step, b)]
            rows.append((0 if kind == "E" else 1, x, y, z))
    return np.asarray(rows, np.int32)


def per_device(tokens, w_query, w_key, w_value, block_order):
    ctx, head = lax.axis_index("ctx"), lax.axis_index("head")
    early = head // 2
    x, y, z = ctx // 32, (ctx // 8) % 4, ctx % 8
    rel = origins()
    from_ctx = (((x - rel[:, 1]) % 2) * 4 + (y - rel[:, 2]) % 4) * 8 + (z - rel[:, 3]) % 8
    index = from_ctx * 2 + (rel[:, 0] + early) % 2
    blocks = jnp.arange(128, dtype=jnp.int32)
    place = jnp.sum(jnp.where(index[:, None] == blocks[None, :], block_order[None, :], 0), 1)
    own = [lax.dynamic_index_in_dim(block_order, ctx * 2 + (part + early) % 2, 0, False) for part in range(2)]
    lanes = jnp.arange(HD, dtype=jnp.int32)[None, :]
    bound = jnp.where(lanes == 0, own[0], jnp.where(lanes == 1, own[1], 1 << 20))
    aug = jnp.where(place[:, None] < bound, 0.0, LOW).astype(jnp.bfloat16)
    aug = jnp.broadcast_to(aug[:, None, :], (128, 16, HD)).reshape(STEPS, 2 * PAIRS, 16, HD)
    table = rotary_table(16384)
    table = jnp.concatenate([lax.dynamic_slice_in_dim(table, b, 1, 0) for b in own], 0)
    anywhere, vmem = pl.BlockSpec(memory_space=pl.ANY), pl.BlockSpec(memory_space=pltpu.VMEM)
    count = len(MESSAGES)
    return pl.pallas_call(
        kernel,
        out_shape=jax.ShapeDtypeStruct((256, 1024), jnp.bfloat16),
        in_specs=[anywhere] * 4 + [vmem] * 2,
        out_specs=vmem,
        scratch_shapes=[
            pltpu.VMEM((2, 128, 4096), jnp.bfloat16),
            pltpu.VMEM((4096, 1024), jnp.bfloat16),
            pltpu.VMEM((4096, 256), jnp.bfloat16),
            pltpu.VMEM((2048, HD), jnp.bfloat16),
            pltpu.VMEM((STEPS, 2, 1024, HD), jnp.bfloat16),
            pltpu.VMEM((2048, HD), jnp.float32),
            pltpu.VMEM((2048, 2 * HD), jnp.float32),
            pltpu.SemaphoreType.DMA((count,)),
            pltpu.SemaphoreType.DMA((count,)),
            pltpu.SemaphoreType.DMA((10,)),
            pltpu.SemaphoreType.DMA((8,)),
            pltpu.SemaphoreType.DMA((7,)),
        ],
        compiler_params=pltpu.CompilerParams(
            collective_id=0, has_side_effects=True, vmem_limit_bytes=56 << 20
        ),
        cost_estimate=pl.CostEstimate(flops=38 * 10**9, bytes_accessed=12 * 10**6, transcendentals=33 * 10**6),
    )(tokens, w_query, w_key, w_value, table, aug)


def solution(mesh):
    return jax.shard_map(
        per_device,
        mesh=mesh,
        in_specs=(P(("ctx", "head"), None), P(None, "head"), P(None, "head"), P(None, "head"), P()),
        out_specs=P("ctx", "head"),
        check_vma=False,
    )
```

time: 1240 us -> 104 us (0.08)
  the two profiles are of different devices: /device:TPU:250 before, /device:TPU:1 now
where the time goes in v1:
time: 104 us
  Pallas kernels  91.4 us (88%)
  local copies, waits for them, and re-layouts  5.02 us (5%)
  between operations  3.65 us (4%)
  other arithmetic  3.52 us (3%)
    pallas_call x1, Pallas kernels, per_device(): pl.pallas_call(kernel, out_shape=jax.ShapeDtypeStruct((256, 1024), jnp.bf...  91.4 us

profile of v1, /device:TPU:1, one launch (start us, length us, event | category | flops | bytes accessed | tf_op | source)
XLA Modules:
  0.0 103.6 jit_solution(2481605305961465648)
XLA Ops:
  0.0 1.3 %fusion.10 = (s32[1]{0:T(128)}, s32[1]{0:T(128)}) fusion(s32[128]{0:T(128)} %param.14, s32[]{:T(128)S(6)} %select_n.92, s32[]{:T(128)S(6)} %select_n.95), kind=kLoop, calls=%fused_computation.30 | loop fusion | bytes 24 | tf_op jit(solution)/shard_map/jit(dynamic_index_in_dim)/dynamic_slice | solution.py:352
  4.9 1.9 %compare_select_fusion.9 = (s32[128]{0:T(128)S(1)}, s32[128]{0:T(128)S(1)}) fusion(s32[]{:T(128)} %bitcast.1, s32[]{:T(128)} %bitcast, s32[128]{0:T(128)} %constant.133.clone, s32[]{:T(128)S(6)} %select_n.90, s32[128]{0:T(128)} %constant.138, s32[]{:T(128)S(6)} %select_n.102, s32[128]{0:T(128)} %constant.137, s32[]{:T(128)S(6)} %select_n.100, ...), kind=kLoop, calls=%fused_computation.13 | loop fusion | flops 7424 | bytes 3096 | tf_op jit(solution)/shard_map/jit(_where)/select_n | solution.py:354
  6.9 0.8 select_reduce_fusion
  7.7 0.1 lt.80
  7.8 0.1 select_convert_fusion
  7.9 0.9 constant_dynamic-slice_fusion.1
  8.8 0.7 pad_maximum_fusion.table
  9.4 0.9 broadcast_in_dim.50.aug
  10.3 91.4 %shard_map.100 = bf16[256,1024]{1,0:T(8,128)(2,1)} custom-call(bf16[64,4096]{1,0:T(8,128)(2,1)} %tok_in.1, bf16[4096,1024]{1,0:T(8,128)(2,1)} %wq_in.1, bf16[4096,128]{1,0:T(8,128)(2,1)} %wk_in.1, bf16[4096,128]{1,0:T(8,128)(2,1)} %wv_in.1, f32[2,128,128]{2,1,0:T(8,128)} %pad_maximum_fusion.table, bf16[16,8,16,128]{3,2,1,0:T(8,128)(2,1)} %broadcast_in_dim.50.aug), custom_call_target="tpu_custom_call" | custom-call | flops 38000001024 | bytes 12000000 | tf_op jit(solution)/shard_map/pallas_call | solution.py:361
  101.7 1.9 %copy.12 = bf16[256,1024]{1,0:T(8,128)(2,1)} copy(bf16[256,1024]{1,0:T(8,128)(2,1)} %shard_map.100) | data formatting | bytes 1048576

commit v2 on v1

v2 whole, which is shorter than its diff:
```python
import math

import jax
import jax.numpy as jnp
import numpy as np
from jax import lax
from jax.experimental import pallas as pl
from jax.experimental.pallas import tpu as pltpu
from jax.sharding import PartitionSpec as P

HD = 128
BLK = 128
NX, NY, NZ = 2, 4, 8
CHUNKS = 16
ROWS = 1024
HALF = 64
TILE = 512
WIDE = 256
AHEAD = 1
LOW = -1e30
FACTOR = math.log2(math.e) / math.sqrt(HD)
CONTRACT_LAST = (((1,), (1,)), ((), ()))
MOVES = {"x": (1, 0, 0), "y+": (0, 1, 0), "y-": (0, -1, 0), "z+": (0, 0, 1), "z-": (0, 0, -1)}
KINDS = {"E": ("E1", "E2"), "L": ("L1", "L2")}
YS = (0, 1, 3, 2)
ZS = (0, 1, 7, 2, 6, 3, 5, 4)
BACKLOG = 3.0
PATHS = {"E1": "xzy", "E2": "zyx", "L1": "yzx", "L2": "xzy"}
FIRST = [
    ("L1", "y"), ("L2", "x"), ("E2", "z"), ("E1", "z"), ("E2", "y"), ("L1", "x"),
    ("L1", "z"), ("L2", "y"), ("E2", "x"), ("E1", "y"), ("L2", "z"), ("E1", "x"),
]


def moved(item, way):
    kind, x, y, z = item
    dx, dy, dz = MOVES[way]
    return (kind, (x + dx) % NX, (y + dy) % NY, (z + dz) % NZ)


def run(kind, xs, ys, zs):
    return [(kind, x, y, z) for y in ys for z in zs for x in xs]


def all_groups():
    out = []
    for kind, path in PATHS.items():
        sides = [(0, 1)] if path[0] == "x" else [(0,), (1,)]
        for xs in sides:
            if path.index("y") < path.index("z"):
                for z in range(NZ):
                    out += [run(kind, xs, ys, (z,)) for ys in (YS[:2], YS[2:])]
            else:
                for y in range(NY):
                    out += [run(kind, xs, (y,), ZS[n : n + 2]) for n in (0, 2, 4, 6)]
    return out


def first_y(kind, xs):
    out = [(way, run(kind, (x,), (0,), (0,))) for x in xs for way in ("y+", "y-")]
    out.append(("y+", run(kind, (0,), (1,), (0,))))
    return out + ([("y-", run(kind, (1,), (3,), (0,)))] if len(xs) > 1 else [])


def first_z(kind, xs):
    out = [(way, run(kind, (x,), (0,), (0,))) for x in xs for way in ("z+", "z-")]
    for up, down in ((1, 7), (2, 6)):
        out += [("z+", run(kind, xs, (0,), (up,))), ("z-", run(kind, xs, (0,), (down,)))]
    out.append(("z+", run(kind, (0,), (0,), (3,))))
    return out + ([("z-", run(kind, (1,), (0,), (5,)))] if len(xs) > 1 else [])


def along_z(kind, xs):
    out = []
    for up, down in ((0, 0), (1, 7), (2, 6)):
        for ys in (YS[:1], YS[1:2], YS[2:]):
            out += [("z+", run(kind, xs, ys, (up,))), ("z-", run(kind, xs, ys, (down,)))]
    out.append(("z+", run(kind, xs, YS[:2], (3,))))
    return out + [("z-", run(kind, xs, YS[2:], (5,)))]


def along_y(kind, xs):
    out = []
    for zs in (ZS[:1], ZS[1:2], ZS[2:4], ZS[4:6], ZS[6:]):
        out += [(way, run(kind, xs, (0,), zs)) for way in ("y+", "y-")]
    for zs in (ZS[:2], ZS[2:4]):
        out.append(("y+", run(kind, xs, (1,), zs)))
    for zs in (ZS[4:6], ZS[6:]):
        out.append(("y-", run(kind, xs, (3,), zs)))
    return out


def stages(kind):
    path, both = PATHS[kind], (0, 1)
    xs = both if path[0] == "x" else (0,)
    if path.index("y") < path.index("z"):
        first, then = ("y", first_y(kind, xs)), ("z", along_z(kind, xs))
        rows = [run(kind, (0,), ys, (z,)) for z in ZS for ys in (YS[:2], YS[2:])]
    else:
        first, then = ("z", first_z(kind, xs)), ("y", along_y(kind, xs))
        rows = [run(kind, (0,), (y,), ZS[n : n + 2]) for y in YS for n in (0, 2, 4, 6)]
    if path[0] == "x":
        rows = [run(kind, (0,), (0,), (0,))]
    return dict([first, then, ("x", [("x", items) for items in rows])])


def all_messages():
    return [message for kind, axis in FIRST for message in stages(kind)[axis]]


def plan():
    messages, groups = all_messages(), all_groups()
    half_us, latency = 0.71, 2.8
    segments = [("qE", 0.6)] * 4 + [("ownE", 0.4)] + [("ahead", 1.25)] * AHEAD
    segments += [("kvL", 0.8)] + [("qL", 0.6)] * 4 + [("ownL", 0.4)]
    segments += [("step", 2.5)] * (CHUNKS - AHEAD)
    have = {("E1", 0, 0, 0), ("E2", 0, 0, 0)}
    free = {way: 0.0 for way in MOVES}
    arrival, unsent, arrived, left = {}, list(range(len(messages))), set(), list(range(len(groups)))
    complete = {}
    now = 2.5
    actions, order = [], []

    def send_ready(acts):
        for m in list(unsent):
            way, items = messages[m]
            if free[way] <= now + BACKLOG and all(item in have for item in items):
                unsent.remove(m)
                free[way] = max(now, free[way]) + half_us * len(items)
                arrival[m] = free[way] + latency
                acts.append(("send", m))

    def note():
        for g in left:
            if g not in complete and all(item in have for item in groups[g]):
                complete[g] = len(complete)

    def take(m, acts):
        nonlocal now
        acts.append(("wait", m))
        now = max(now, arrival[m])
        arrived.add(m)
        have.update(moved(item, messages[m][0]) for item in messages[m][1])
        note()
        send_ready(acts)

    def pending():
        return sorted((arrival[m], m) for m in arrival if m not in arrived)

    def choose(ready, room):
        if room == 0:
            return []
        for n, g in enumerate(ready):
            if len(groups[g]) <= room:
                rest = choose(ready[n + 1 :], room - len(groups[g]))
                if rest is not None:
                    return [g] + rest
        return None

    def chosen_now():
        ready = sorted((g for g in left if g in complete), key=complete.get)
        return choose(ready, ROWS // HALF) if sum(len(groups[g]) for g in ready) >= ROWS // HALF else None

    for what, length in segments:
        acts = []
        if what == "kvL":
            now = max(now, 16.0)
        send_ready(acts)
        while True:
            soon = [(t, m) for t, m in pending() if t <= now]
            if not soon:
                break
            take(soon[0][1], acts)
        if what in ("step", "ahead"):
            while (chosen := chosen_now()) is None:
                take(pending()[0][1], acts)
            for g in chosen:
                left.remove(g)
            order.append(chosen)
        actions.append((what, acts))
        now += length
        if what == "kvL":
            have.update([("L1", 0, 0, 0), ("L2", 0, 0, 0)])
    assert not left and len(arrived) == len(messages)
    place = {}
    for chunk, chosen in enumerate(order):
        row = 0
        for g in chosen:
            for item in groups[g]:
                place[item] = (chunk, row)
                row += HALF
        assert row == ROWS
    return messages, actions, place, now


MESSAGES, ACTIONS, PLACE, ESTIMATE = plan()


def kernel(
    tok_in, wq_in, wk_in, wv_in, blocks, base, offset, out,
    tok, wq, wkv, query, kv, aug, largest, acc,
    send, recv, tok_sem, relay_sem, local,
):
    ctx, head = lax.axis_index("ctx"), lax.axis_index("head")
    x, y, z = ctx // 32, (ctx // 8) % 4, ctx % 8
    early, core = head // 2, head % 2

    def device(x, y, z):
        return ((x * 4 + y) * 8 + z, head)

    near = {
        "x": device(1 - x, y, z),
        "y+": device(x, (y + 1) % 4, z),
        "y-": device(x, (y + 3) % 4, z),
        "z+": device(x, y, (z + 1) % 8),
        "z-": device(x, y, (z + 7) % 8),
    }
    beside = (ctx, head + 1 - 2 * core)
    across = (ctx, (head + 2) % 4)

    barrier = pltpu.get_barrier_semaphore()
    peers = list(near.values()) + [beside, across]
    for peer in peers:
        pl.semaphore_signal(barrier, inc=1, device_id=peer, device_id_type=pl.DeviceIdType.MESH)

    mine = pl.ds(pl.multiple_of(core * 64, 64), 64)
    own_tokens = pltpu.make_async_copy(tok_in, tok.at[0, mine], local.at[2])
    own_tokens.start()
    copies = [
        pltpu.make_async_copy(wk_in, wkv.at[:, 0:HD], local.at[0]),
        pltpu.make_async_copy(wv_in, wkv.at[:, HD : 2 * HD], local.at[1]),
    ]
    for copy in copies:
        copy.start()
    wide = []
    for j in range(4):
        columns = pl.ds(j * WIDE, WIDE)
        wide.append(pltpu.make_async_copy(wq_in.at[:, columns], wq.at[:, columns], local.at[3 + j]))
        wide[-1].start()
    pl.semaphore_wait(barrier, len(peers))

    def remote(src, dst, s, r, to):
        return pltpu.make_async_remote_copy(
            src_ref=src, dst_ref=dst, send_sem=s, recv_sem=r, device_id=to,
            device_id_type=pl.DeviceIdType.MESH,
        )

    to_beside = remote(tok_in, tok.at[0, mine], tok_sem.at[0], tok_sem.at[1], beside)
    to_beside.start()
    to_across, relays = [], []
    for j in range(4):
        rows = pl.ds(pl.multiple_of(core * 64 + j * 16, 16), 16)
        to_across.append(
            remote(tok_in.at[pl.ds(j * 16, 16)], tok.at[1, rows], tok_sem.at[2 + j], tok_sem.at[6 + j], across)
        )
        relays.append(
            remote(tok.at[1, rows], tok.at[1, rows], relay_sem.at[j], relay_sem.at[4 + j], beside)
        )

    to_across[0].start()

    own = [blocks[ctx * 2 + early], blocks[ctx * 2 + 1 - early]]
    lanes = lax.broadcasted_iota(jnp.int32, (16, HD), 1)
    bound = jnp.where(lanes == 0, own[0], jnp.where(lanes == 1, own[1], 1 << 20))
    for dx in range(NX):
        for dy in range(NY):
            for dz in range(NZ):
                origin = (((x + dx) % NX) * 4 + (y - dy + NY) % NY) * 8 + (z - dz + NZ) % NZ
                for part, kinds in ((early, KINDS["E"]), (1 - early, KINDS["L"])):
                    place = blocks[origin * 2 + part]
                    mask = jnp.where(place < bound, 0.0, LOW).astype(jnp.bfloat16)
                    for kind in kinds:
                        chunk, row = PLACE[(kind, dx, dy, dz)]
                        aug[chunk, row // HALF] = mask

    def slot(items):
        chunk, row = PLACE[items[0]]
        count = len(items) * HALF
        spots = [PLACE[item] for item in items]
        assert spots == [(chunk, row + n * HALF) for n in range(len(items))]
        return kv.at[chunk, :, pl.ds(row, count)]

    def message(m):
        way, items = MESSAGES[m]
        landing = [moved(item, way) for item in items]
        return remote(slot(items), slot(landing), send.at[m], recv.at[m], near[way])

    def communicate(acts):
        for what, m in acts:
            if what == "send":
                message(m).start()
            else:
                message(m).wait_recv()

    def rotation(part):
        turn = own[part]
        base_cos, base_sin = base[0, pl.ds(turn, 1)], base[1, pl.ds(turn, 1)]
        cosine = base_cos * offset[0] - base_sin * offset[1]
        sine = base_sin * offset[0] + base_cos * offset[1]
        return lambda values: (values * cosine + pltpu.roll(values, HD // 2, 1) * sine).astype(jnp.bfloat16)

    def project_kv(part, spots):
        both = jnp.dot(tok[part], wkv[...], preferred_element_type=jnp.float32)
        keys, values = rotation(part)(both[:, :HD]), both[:, HD:].astype(jnp.bfloat16)
        size = BLK // len(spots)
        for n, item in enumerate(spots):
            chunk, row = PLACE[item]
            kv[chunk, 0, pl.ds(row, size)] = keys[n * size : (n + 1) * size]
            kv[chunk, 1, pl.ds(row, size)] = values[n * size : (n + 1) * size]

    def project_q(part, j):
        both = jnp.dot(tok[part], wq[:, j * WIDE : (j + 1) * WIDE], preferred_element_type=jnp.float32)
        rotate = rotation(part)
        for h in range(2):
            rows = pl.ds(part * ROWS + (2 * j + h) * BLK, BLK)
            query[rows] = rotate(both[:, h * HD : (h + 1) * HD])

    lane = lax.broadcasted_iota(jnp.int32, (TILE, HD), 1)
    marks = [jnp.where(lane == part, 1.0, 0.0).astype(jnp.bfloat16) for part in range(2)]

    def own_block(part, spots):
        ones = jnp.ones((BLK, HD), jnp.bfloat16)
        row = lax.broadcasted_iota(jnp.int32, (TILE, BLK), 0) % BLK
        keep = lax.broadcasted_iota(jnp.int32, (TILE, BLK), 1) <= row
        size = BLK // len(spots)
        at = [PLACE[item] for item in spots]
        keys, values = (
            jnp.concatenate([kv[chunk, n, pl.ds(row, size)] for chunk, row in at], 0) for n in range(2)
        )
        values = jnp.concatenate([values, ones], 1)
        for t in range(ROWS // TILE):
            rows = pl.ds(part * ROWS + t * TILE, TILE)
            scores = lax.dot_general(query[rows], keys, CONTRACT_LAST, preferred_element_type=jnp.float32)
            scores = jnp.where(keep, scores, LOW)
            top = jnp.broadcast_to(jnp.max(scores, axis=1, keepdims=True), (TILE, HD))
            expo = jnp.exp2((scores - top) * FACTOR).astype(jnp.bfloat16)
            largest[rows] = top
            acc[rows] = jnp.dot(expo, values, preferred_element_type=jnp.float32)

    def score(part, rows, chunk):
        masks = [aug[chunk, b] for b in range(ROWS // HALF) for _ in range(HALF // 16)]
        keys = jnp.concatenate([kv[chunk, 0], jnp.concatenate(masks, 0)], 1)
        wide_query = jnp.concatenate([query[rows], marks[part]], 1)
        return lax.dot_general(wide_query, keys, CONTRACT_LAST, preferred_element_type=jnp.float32)

    def weigh(rows, scores):
        before = largest[rows]
        after = jnp.maximum(before, jnp.max(scores, axis=1, keepdims=True))
        largest[rows] = after
        expo = [
            jnp.exp2((scores[:, n : n + HD] - after) * FACTOR).astype(jnp.bfloat16) for n in range(0, ROWS, HD)
        ]
        return jnp.concatenate(expo, 1), jnp.exp2((before - after) * FACTOR)

    def gather(rows, chunk, expo, shrink):
        values = jnp.concatenate([kv[chunk, 1], jnp.ones((ROWS, HD), jnp.bfloat16)], 1)
        product = jnp.dot(expo, values, preferred_element_type=jnp.float32)
        acc[rows] = acc[rows] * jnp.concatenate([shrink, shrink], 1) + product

    def attend(pairs):
        work = [
            (part, pl.ds(part * ROWS + t * TILE, TILE), chunk) for part, chunk in pairs for t in range(ROWS // TILE)
        ]
        scores, weights = {}, {}
        for n in range(len(work) + 2):
            if n < len(work):
                scores[n] = score(*work[n])
            if n >= 2:
                part, rows, chunk = work[n - 2]
                gather(rows, chunk, *weights.pop(n - 2))
            if 1 <= n <= len(work):
                weights[n - 1] = weigh(work[n - 1][1], scores.pop(n - 1))

    own_tokens.wait()
    to_beside.wait_recv()
    for copy in copies:
        copy.wait()
    spots = [[(kind, 0, 0, 0) for kind in KINDS[part]] for part in "EL"]
    project_kv(0, spots[0])
    step_acts = []
    count = {what: 0 for what, _ in ACTIONS}
    for what, acts in ACTIONS:
        n = count[what]
        count[what] += 1
        if what == "step":
            step_acts.append(acts)
            continue
        communicate(acts)
        if what == "qE" and n == 0:
            for k in range(1, 4):
                to_across[k].start()
        if what == "qE":
            wide[n].wait()
            project_q(0, n)
        elif what == "ownE":
            own_block(0, spots[0])
        elif what == "ahead":
            attend([(0, n)])
        elif what == "kvL":
            for k in range(4):
                to_across[k].wait_recv()
                relays[k].start()
            for k in range(4):
                relays[k].wait_recv()
            project_kv(1, spots[1])
        elif what == "qL":
            project_q(1, n)
        else:
            own_block(1, spots[1])

    def one_step(step, carry):
        for s, acts in enumerate(step_acts):
            if acts:

                @pl.when(step == s)
                def _(acts=acts):
                    communicate(acts)

        attend([(1, step), (0, step + AHEAD)])
        return carry

    lax.fori_loop(0, CHUNKS - AHEAD, one_step, 0)
    attend([(1, chunk) for chunk in range(CHUNKS - AHEAD, CHUNKS)])

    for part in range(2):
        block = pl.ds(pl.multiple_of((early if part == 0 else 1 - early) * BLK, BLK), BLK)
        for h in range(8):
            rows = pl.ds(part * ROWS + h * BLK, BLK)
            total = acc[rows]
            out[block, h * HD : (h + 1) * HD] = (total[:, :HD] / total[:, HD:]).astype(jnp.bfloat16)

    for m in range(len(MESSAGES)):
        message(m).wait_send()
    to_beside.wait_send()
    for k in range(4):
        to_across[k].wait_send()
        relays[k].wait_send()


def rotary_tables():
    freqs = 500000.0 ** (-(np.arange(HD // 2) * 2.0) / HD)
    out = []
    for positions in (np.arange(128.0) * BLK, np.arange(float(BLK))):
        angles = positions[:, None] * freqs[None, :]
        cosine, sine = np.cos(angles), np.sin(angles)
        joined = [np.concatenate([cosine, cosine], 1), np.concatenate([-sine, sine], 1)]
        out.append(jnp.asarray(np.stack(joined), jnp.float32))
    return out


def per_device(tokens, w_query, w_key, w_value, block_order):
    anywhere, vmem = pl.BlockSpec(memory_space=pl.ANY), pl.BlockSpec(memory_space=pltpu.VMEM)
    count = len(MESSAGES)
    return pl.pallas_call(
        kernel,
        out_shape=jax.ShapeDtypeStruct((256, 1024), jnp.bfloat16),
        in_specs=[anywhere] * 4 + [pl.BlockSpec(memory_space=pltpu.SMEM), vmem, vmem],
        out_specs=vmem,
        scratch_shapes=[
            pltpu.VMEM((2, 128, 4096), jnp.bfloat16),
            pltpu.VMEM((4096, 1024), jnp.bfloat16),
            pltpu.VMEM((4096, 256), jnp.bfloat16),
            pltpu.VMEM((2048, HD), jnp.bfloat16),
            pltpu.VMEM((CHUNKS, 2, ROWS, HD), jnp.bfloat16),
            pltpu.VMEM((CHUNKS, ROWS // HALF, 16, HD), jnp.bfloat16),
            pltpu.VMEM((2048, HD), jnp.float32),
            pltpu.VMEM((2048, 2 * HD), jnp.float32),
            pltpu.SemaphoreType.DMA((count,)),
            pltpu.SemaphoreType.DMA((count,)),
            pltpu.SemaphoreType.DMA((10,)),
            pltpu.SemaphoreType.DMA((8,)),
            pltpu.SemaphoreType.DMA((7,)),
        ],
        compiler_params=pltpu.CompilerParams(
            collective_id=0, has_side_effects=True, vmem_limit_bytes=56 << 20
        ),
        cost_estimate=pl.CostEstimate(flops=38 * 10**9, bytes_accessed=12 * 10**6, transcendentals=33 * 10**6),
    )(tokens, w_query, w_key, w_value, block_order, *rotary_tables())


def solution(mesh):
    return jax.shard_map(
        per_device,
        mesh=mesh,
        in_specs=(P(("ctx", "head"), None), P(None, "head"), P(None, "head"), P(None, "head"), P()),
        out_specs=P("ctx", "head"),
        check_vma=False,
    )
```

time: 104 us -> 84.5 us (0.81)
  Pallas kernels: 91.4 us -> 82.4 us
  between operations: 3.65 us -> 0.01 us
  other arithmetic: 3.52 us -> 0 us
  local copies, waits for them, and re-layouts: 5.02 us -> 1.87 us
    pallas_call x1, Pallas kernels: 91.4 us -> 82.4 us  [per_device(): pl.pallas_call(kernel, out_shape=jax.ShapeDtypeStruct((256, 1024), jnp.bf...]
    dynamic_slice x2 -> x0, local copies, waits for them, and re-layouts: 2.2 us -> none  [the longest x1 1.31 us: per_device(): lax.dynamic_index_in_dim(block_order, ctx * 2 + (part + early) % 2, 0, Fa...]
    select_n x1 -> x0, other arithmetic: 1.93 us -> none  [per_device(): jnp.where(lanes == 0, own[0], jnp.where(lanes == 1, own[1], 1 << 20))]
where the time goes in v2:
time: 84.5 us; the launch traced here: 84.3 us
  Pallas kernels  82.4 us (98%)
  local copies, waits for them, and re-layouts  1.87 us (2%)
    pallas_call x1, Pallas kernels, per_device(): pl.pallas_call(kernel, out_shape=jax.ShapeDtypeStruct((256, 1024), jnp.bf...  82.4 us
    unnamed x1, local copies, waits for them, and re-layouts  1.87 us

profile of v2, /device:TPU:1, one launch (start us, length us, event | category | flops | bytes accessed | tf_op | source)
XLA Modules:
  0.0 84.3 jit_solution(3053108351107430180)
XLA Ops:
  0.0 82.4 %shard_map.73 = bf16[256,1024]{1,0:T(8,128)(2,1)} custom-call(bf16[64,4096]{1,0:T(8,128)(2,1)} %tok_in.1, bf16[4096,1024]{1,0:T(8,128)(2,1)} %wq_in.1, bf16[4096,128]{1,0:T(8,128)(2,1)} %wk_in.1, bf16[4096,128]{1,0:T(8,128)(2,1)} %wv_in.1, s32[128]{0:T(128)} %blocks.1, f32[2,128,128]{2,1,0:T(8,128)} %constant.4.clone.base, f32[2,128,128]{2,1,0:T(8,128)} %constant.5.clone.offset), custom_call_target="tpu_custom_call" | custom-call | flops 38000001024 | bytes 12000000 | tf_op jit(solution)/shard_map/pallas_call | solution.py:454
  82.5 1.9 %copy.9 = bf16[256,1024]{1,0:T(8,128)(2,1)} copy(bf16[256,1024]{1,0:T(8,128)(2,1)} %shard_map.73) | data formatting | bytes 1048576

commit v3 on v2

--- a/solution.py
+++ b/solution.py
@@ -16,19 +16,24 @@
 HALF = 64
 TILE = 512
 WIDE = 256
-AHEAD = 1
+AHEAD = 0
 LOW = -1e30
 FACTOR = math.log2(math.e) / math.sqrt(HD)
 CONTRACT_LAST = (((1,), (1,)), ((), ()))
-MOVES = {"x": (1, 0, 0), "y+": (0, 1, 0), "y-": (0, -1, 0), "z+": (0, 0, 1), "z-": (0, 0, -1)}
+MOVES = {
+    "x": (1, 0, 0), "y+": (0, 1, 0), "y-": (0, -1, 0), "z+": (0, 0, 1), "z-": (0, 0, -1),
+    "y2": (0, 2, 0), "z+2": (0, 0, 2), "z-2": (0, 0, -2),
+}
+LOADS = {"y2": {"y+": 1, "y-": 1}, "z+2": {"z+": 2}, "z-2": {"z-": 2}}
 KINDS = {"E": ("E1", "E2"), "L": ("L1", "L2")}
 YS = (0, 1, 3, 2)
 ZS = (0, 1, 7, 2, 6, 3, 5, 4)
 BACKLOG = 3.0
-PATHS = {"E1": "xzy", "E2": "zyx", "L1": "yzx", "L2": "xzy"}
+PATHS = {"E1": "xzy", "E2": "yzx", "L1": "xzy", "L2": "xyz"}
+FAR = ("E1", "E2", "L1", "L2",)
 FIRST = [
-    ("L1", "y"), ("L2", "x"), ("E2", "z"), ("E1", "z"), ("E2", "y"), ("L1", "x"),
-    ("L1", "z"), ("L2", "y"), ("E2", "x"), ("E1", "y"), ("L2", "z"), ("E1", "x"),
+    ("E2", "x"), ("L2", "y"), ("L2", "x"), ("E1", "y"), ("L1", "x"), ("E1", "x"),
+    ("L2", "z"), ("L1", "z"), ("E2", "z"), ("E2", "y"), ("L1", "y"), ("E1", "z"),
 ]
 
 
@@ -56,14 +61,21 @@
     return out
 
 
-def first_y(kind, xs):
+def first_y(kind, xs, far):
     out = [(way, run(kind, (x,), (0,), (0,))) for x in xs for way in ("y+", "y-")]
+    if far:
+        return out + [("y2", run(kind, (x,), (0,), (0,))) for x in xs]
     out.append(("y+", run(kind, (0,), (1,), (0,))))
     return out + ([("y-", run(kind, (1,), (3,), (0,)))] if len(xs) > 1 else [])
 
 
-def first_z(kind, xs):
+def first_z(kind, xs, far):
     out = [(way, run(kind, (x,), (0,), (0,))) for x in xs for way in ("z+", "z-")]
+    if far:
+        out += [(way, run(kind, (x,), (0,), (0,))) for x in xs for way in ("z+2", "z-2")]
+        out += [("z+", run(kind, xs, (0,), (2,))), ("z-", run(kind, xs, (0,), (6,)))]
+        out.append(("z+2", run(kind, (0,), (0,), (2,))))
+        return out + ([("z-2", run(kind, (1,), (0,), (6,)))] if len(xs) > 1 else [])
     for up, down in ((1, 7), (2, 6)):
         out += [("z+", run(kind, xs, (0,), (up,))), ("z-", run(kind, xs, (0,), (down,)))]
     out.append(("z+", run(kind, (0,), (0,), (3,))))
@@ -94,10 +106,10 @@
     path, both = PATHS[kind], (0, 1)
     xs = both if path[0] == "x" else (0,)
     if path.index("y") < path.index("z"):
-        first, then = ("y", first_y(kind, xs)), ("z", along_z(kind, xs))
+        first, then = ("y", first_y(kind, xs, kind in FAR)), ("z", along_z(kind, xs))
         rows = [run(kind, (0,), ys, (z,)) for z in ZS for ys in (YS[:2], YS[2:])]
     else:
-        first, then = ("z", first_z(kind, xs)), ("y", along_y(kind, xs))
+        first, then = ("z", first_z(kind, xs, kind in FAR)), ("y", along_y(kind, xs))
         rows = [run(kind, (0,), (y,), ZS[n : n + 2]) for y in YS for n in (0, 2, 4, 6)]
     if path[0] == "x":
         rows = [run(kind, (0,), (0,), (0,))]
@@ -110,24 +122,31 @@
 
 def plan():
     messages, groups = all_messages(), all_groups()
-    half_us, latency = 0.71, 2.8
-    segments = [("qE", 0.6)] * 4 + [("ownE", 0.4)] + [("ahead", 1.25)] * AHEAD
-    segments += [("kvL", 0.8)] + [("qL", 0.6)] * 4 + [("ownL", 0.4)]
-    segments += [("step", 2.5)] * (CHUNKS - AHEAD)
+    half_us, latency, issue_us, margin = 0.82, 2.8, 0.02, 0.4
+    segments = [("qE", 0.6)] * 4 + [("ownE", 0.4)] + [("part", 0.8)] * 3 + [("ahead", 1.4)] * AHEAD
+    segments += [("kvL", 0.5), ("qL", 1.2), ("ownL", 0.4)]
+    segments += [("step", 2.75)] * (CHUNKS - AHEAD)
+    tokens_at = [16.0, 12.5, 9.5, 6.5]
     have = {("E1", 0, 0, 0), ("E2", 0, 0, 0)}
-    free = {way: 0.0 for way in MOVES}
+    free = {way: 0.0 for way in MOVES if way not in LOADS}
     arrival, unsent, arrived, left = {}, list(range(len(messages))), set(), list(range(len(groups)))
     complete = {}
     now = 2.5
     actions, order = [], []
 
     def send_ready(acts):
+        nonlocal now
         for m in list(unsent):
             way, items = messages[m]
-            if free[way] <= now + BACKLOG and all(item in have for item in items):
+            loads = LOADS.get(way, {way: 1})
+            start = max(free[link] for link in loads)
+            if start <= now + BACKLOG and all(item in have for item in items):
                 unsent.remove(m)
-                free[way] = max(now, free[way]) + half_us * len(items)
-                arrival[m] = free[way] + latency
+                now += issue_us
+                start = max(now, start)
+                for link, load in loads.items():
+                    free[link] = start + half_us * len(items) * load
+                arrival[m] = max(free[link] for link in loads) + latency + (0.7 if way in LOADS else 0.0)
                 acts.append(("send", m))
 
     def note():
@@ -138,7 +157,7 @@
     def take(m, acts):
         nonlocal now
         acts.append(("wait", m))
-        now = max(now, arrival[m])
+        now = max(now, arrival[m]) + issue_us
         arrived.add(m)
         have.update(moved(item, messages[m][0]) for item in messages[m][1])
         note()
@@ -163,11 +182,13 @@
 
     for what, length in segments:
         acts = []
-        if what == "kvL":
-            now = max(now, 16.0)
+        if what in ("part", "kvL"):
+            now = max(now, tokens_at.pop())
         send_ready(acts)
+        if not actions:
+            free["x"] += 9.0
         while True:
-            soon = [(t, m) for t, m in pending() if t <= now]
+            soon = [(t, m) for t, m in pending() if t <= now - margin]
             if not soon:
                 break
             take(soon[0][1], acts)
@@ -198,7 +219,7 @@
 
 def kernel(
     tok_in, wq_in, wk_in, wv_in, blocks, base, offset, out,
-    tok, wq, wkv, query, kv, aug, largest, acc,
+    tok, wq, wkv, query, kv, aug, largest, acc, late,
     send, recv, tok_sem, relay_sem, local,
 ):
     ctx, head = lax.axis_index("ctx"), lax.axis_index("head")
@@ -214,6 +235,9 @@
         "y-": device(x, (y + 3) % 4, z),
         "z+": device(x, y, (z + 1) % 8),
         "z-": device(x, y, (z + 7) % 8),
+        "y2": device(x, (y + 2) % 4, z),
+        "z+2": device(x, y, (z + 2) % 8),
+        "z-2": device(x, y, (z + 6) % 8),
     }
     beside = (ctx, head + 1 - 2 * core)
     across = (ctx, (head + 2) % 4)
@@ -249,14 +273,13 @@
     to_beside.start()
     to_across, relays = [], []
     for j in range(4):
-        rows = pl.ds(pl.multiple_of(core * 64 + j * 16, 16), 16)
+        piece = pl.ds(j * ROWS, ROWS)
         to_across.append(
-            remote(tok_in.at[pl.ds(j * 16, 16)], tok.at[1, rows], tok_sem.at[2 + j], tok_sem.at[6 + j], across)
+            remote(tok_in.at[:, piece], tok.at[1, mine, piece], tok_sem.at[2 + j], tok_sem.at[6 + j], across)
         )
         relays.append(
-            remote(tok.at[1, rows], tok.at[1, rows], relay_sem.at[j], relay_sem.at[4 + j], beside)
+            remote(tok.at[1, mine, piece], tok.at[1, mine, piece], relay_sem.at[j], relay_sem.at[4 + j], beside)
         )
-
     to_across[0].start()
 
     own = [blocks[ctx * 2 + early], blocks[ctx * 2 + 1 - early]]
@@ -299,31 +322,45 @@
         sine = base_sin * offset[0] + base_cos * offset[1]
         return lambda values: (values * cosine + pltpu.roll(values, HD // 2, 1) * sine).astype(jnp.bfloat16)
 
-    def project_kv(part, spots):
-        both = jnp.dot(tok[part], wkv[...], preferred_element_type=jnp.float32)
+    spots = [[(kind, 0, 0, 0) for kind in KINDS[part]] for part in "EL"]
+
+    def store_kv(part, both):
         keys, values = rotation(part)(both[:, :HD]), both[:, HD:].astype(jnp.bfloat16)
-        size = BLK // len(spots)
-        for n, item in enumerate(spots):
+        size = BLK // len(spots[part])
+        for n, item in enumerate(spots[part]):
             chunk, row = PLACE[item]
             kv[chunk, 0, pl.ds(row, size)] = keys[n * size : (n + 1) * size]
             kv[chunk, 1, pl.ds(row, size)] = values[n * size : (n + 1) * size]
 
-    def project_q(part, j):
-        both = jnp.dot(tok[part], wq[:, j * WIDE : (j + 1) * WIDE], preferred_element_type=jnp.float32)
+    def store_q(part, j, both):
         rotate = rotation(part)
         for h in range(2):
             rows = pl.ds(part * ROWS + (2 * j + h) * BLK, BLK)
             query[rows] = rotate(both[:, h * HD : (h + 1) * HD])
 
+    def late_part(k, js):
+        piece = pl.ds(k * ROWS, ROWS)
+        for j in js:
+            weights = wkv[piece] if j == 4 else wq[piece, j * WIDE : (j + 1) * WIDE]
+            product = jnp.dot(tok[1, :, piece], weights, preferred_element_type=jnp.float32)
+            if k:
+                product = late[j] + product
+            if k < 3:
+                late[j] = product
+            elif j == 4:
+                store_kv(1, product)
+            else:
+                store_q(1, j, product)
+
     lane = lax.broadcasted_iota(jnp.int32, (TILE, HD), 1)
     marks = [jnp.where(lane == part, 1.0, 0.0).astype(jnp.bfloat16) for part in range(2)]
 
-    def own_block(part, spots):
+    def own_block(part):
         ones = jnp.ones((BLK, HD), jnp.bfloat16)
         row = lax.broadcasted_iota(jnp.int32, (TILE, BLK), 0) % BLK
         keep = lax.broadcasted_iota(jnp.int32, (TILE, BLK), 1) <= row
-        size = BLK // len(spots)
-        at = [PLACE[item] for item in spots]
+        size = BLK // len(spots[part])
+        at = [PLACE[item] for item in spots[part]]
         keys, values = (
             jnp.concatenate([kv[chunk, n, pl.ds(row, size)] for chunk, row in at], 0) for n in range(2)
         )
@@ -375,8 +412,7 @@
     to_beside.wait_recv()
     for copy in copies:
         copy.wait()
-    spots = [[(kind, 0, 0, 0) for kind in KINDS[part]] for part in "EL"]
-    project_kv(0, spots[0])
+    store_kv(0, jnp.dot(tok[0], wkv[...], preferred_element_type=jnp.float32))
     step_acts = []
     count = {what: 0 for what, _ in ACTIONS}
     for what, acts in ACTIONS:
@@ -391,22 +427,29 @@
                 to_across[k].start()
         if what == "qE":
             wide[n].wait()
-            project_q(0, n)
+            columns = slice(n * WIDE, (n + 1) * WIDE)
+            store_q(0, n, jnp.dot(tok[0], wq[:, columns], preferred_element_type=jnp.float32))
         elif what == "ownE":
-            own_block(0, spots[0])
+            own_block(0)
         elif what == "ahead":
             attend([(0, n)])
+        elif what == "part":
+            to_across[n].wait_recv()
+            relays[n].start()
+            if n:
+                relays[n - 1].wait_recv()
+                late_part(n - 1, range(5))
         elif what == "kvL":
-            for k in range(4):
-                to_across[k].wait_recv()
-                relays[k].start()
-            for k in range(4):
-                relays[k].wait_recv()
-            project_kv(1, spots[1])
+            to_across[3].wait_recv()
+            relays[3].start()
+            relays[2].wait_recv()
+            late_part(2, range(5))
+            relays[3].wait_recv()
+            late_part(3, [4])
         elif what == "qL":
-            project_q(1, n)
+            late_part(3, range(4))
         else:
-            own_block(1, spots[1])
+            own_block(1)
 
     def one_step(step, carry):
         for s, acts in enumerate(step_acts):
@@ -465,6 +508,7 @@
             pltpu.VMEM((CHUNKS, ROWS // HALF, 16, HD), jnp.bfloat16),
             pltpu.VMEM((2048, HD), jnp.float32),
             pltpu.VMEM((2048, 2 * HD), jnp.float32),
+            pltpu.VMEM((5, BLK, WIDE), jnp.float32),
             pltpu.SemaphoreType.DMA((count,)),
             pltpu.SemaphoreType.DMA((count,)),
             pltpu.SemaphoreType.DMA((10,)),

time: 84.5 us -> 81.2 us (0.961)
  Pallas kernels: 82.4 us -> 79.2 us
    pallas_call x1, Pallas kernels: 82.4 us -> 79.2 us  [per_device(): pl.pallas_call(kernel, out_shape=jax.ShapeDtypeStruct((256, 1024), jnp.bf...]
where the time goes in v3:
time: 81.2 us; the launch traced here: 81.1 us
  Pallas kernels  79.2 us (98%)
  local copies, waits for them, and re-layouts  1.87 us (2%)
    pallas_call x1, Pallas kernels, per_device(): pl.pallas_call(kernel, out_shape=jax.ShapeDtypeStruct((256, 1024), jnp.bf...  79.2 us
    unnamed x1, local copies, waits for them, and re-layouts  1.87 us

profile of v3, /device:TPU:1, one launch (start us, length us, event | category | flops | bytes accessed | tf_op | source)
XLA Modules:
  0.0 81.1 jit_solution(15724909772513056037)
XLA Ops:
  0.0 79.2 %shard_map.73 = bf16[256,1024]{1,0:T(8,128)(2,1)} custom-call(bf16[64,4096]{1,0:T(8,128)(2,1)} %tok_in.1, bf16[4096,1024]{1,0:T(8,128)(2,1)} %wq_in.1, bf16[4096,128]{1,0:T(8,128)(2,1)} %wk_in.1, bf16[4096,128]{1,0:T(8,128)(2,1)} %wv_in.1, s32[128]{0:T(128)} %blocks.1, f32[2,128,128]{2,1,0:T(8,128)} %constant.4.clone.base, f32[2,128,128]{2,1,0:T(8,128)} %constant.5.clone.offset), custom_call_target="tpu_custom_call" | custom-call | flops 38000001024 | bytes 12000000 | tf_op jit(solution)/shard_map/pallas_call | solution.py:497
  79.2 1.9 %copy.9 = bf16[256,1024]{1,0:T(8,128)(2,1)} copy(bf16[256,1024]{1,0:T(8,128)(2,1)} %shard_map.73) | data formatting | bytes 1048576

commit v4 on v3

--- a/solution.py
+++ b/solution.py
@@ -283,18 +283,20 @@
     to_across[0].start()
 
     own = [blocks[ctx * 2 + early], blocks[ctx * 2 + 1 - early]]
-    lanes = lax.broadcasted_iota(jnp.int32, (16, HD), 1)
-    bound = jnp.where(lanes == 0, own[0], jnp.where(lanes == 1, own[1], 1 << 20))
-    for dx in range(NX):
-        for dy in range(NY):
-            for dz in range(NZ):
-                origin = (((x + dx) % NX) * 4 + (y - dy + NY) % NY) * 8 + (z - dz + NZ) % NZ
-                for part, kinds in ((early, KINDS["E"]), (1 - early, KINDS["L"])):
-                    place = blocks[origin * 2 + part]
-                    mask = jnp.where(place < bound, 0.0, LOW).astype(jnp.bfloat16)
-                    for kind in kinds:
-                        chunk, row = PLACE[(kind, dx, dy, dz)]
-                        aug[chunk, row // HALF] = mask
+
+    def mask_blocks():
+        lanes = lax.broadcasted_iota(jnp.int32, (16, HD), 1)
+        bound = jnp.where(lanes == 0, own[0], jnp.where(lanes == 1, own[1], 1 << 20))
+        for dx in range(NX):
+            for dy in range(NY):
+                for dz in range(NZ):
+                    origin = (((x + dx) % NX) * 4 + (y - dy + NY) % NY) * 8 + (z - dz + NZ) % NZ
+                    for part, kinds in ((early, KINDS["E"]), (1 - early, KINDS["L"])):
+                        place = blocks[origin * 2 + part]
+                        mask = jnp.where(place < bound, 0.0, LOW).astype(jnp.bfloat16)
+                        for kind in kinds:
+                            chunk, row = PLACE[(kind, dx, dy, dz)]
+                            aug[chunk, row // HALF] = mask
 
     def slot(items):
         chunk, row = PLACE[items[0]]
@@ -425,6 +427,7 @@
         if what == "qE" and n == 0:
             for k in range(1, 4):
                 to_across[k].start()
+            mask_blocks()
         if what == "qE":
             wide[n].wait()
             columns = slice(n * WIDE, (n + 1) * WIDE)
@@ -452,13 +455,15 @@
             own_block(1)
 
     def one_step(step, carry):
-        for s, acts in enumerate(step_acts):
-            if acts:
-
-                @pl.when(step == s)
-                def _(acts=acts):
-                    communicate(acts)
-
+        def pick(low, high):
+            if high - low == 1:
+                communicate(step_acts[low])
+            else:
+                middle = (low + high) // 2
+                pl.when(step < middle)(lambda: pick(low, middle))
+                pl.when(step >= middle)(lambda: pick(middle, high))
+
+        pick(0, len(step_acts))
         attend([(1, step), (0, step + AHEAD)])
         return carry
 

time: 81.2 us -> 76.4 us (0.941)
  Pallas kernels: 79.2 us -> 74.4 us
    pallas_call x1, Pallas kernels: 79.2 us -> 74.4 us  [per_device(): pl.pallas_call(kernel, out_shape=jax.ShapeDtypeStruct((256, 1024), jnp.bf...]
where the time goes in v4:
time: 76.4 us; the launch traced here: 76.3 us
  Pallas kernels  74.4 us (97%)
  local copies, waits for them, and re-layouts  1.87 us (2%)
    pallas_call x1, Pallas kernels, per_device(): pl.pallas_call(kernel, out_shape=jax.ShapeDtypeStruct((256, 1024), jnp.bf...  74.4 us
    unnamed x1, local copies, waits for them, and re-layouts  1.87 us

profile of v4, /device:TPU:1, one launch (start us, length us, event | category | flops | bytes accessed | tf_op | source)
XLA Modules:
  0.0 76.3 jit_solution(3223570102202892742)
XLA Ops:
  0.0 74.4 %shard_map.73 = bf16[256,1024]{1,0:T(8,128)(2,1)} custom-call(bf16[64,4096]{1,0:T(8,128)(2,1)} %tok_in.1, bf16[4096,1024]{1,0:T(8,128)(2,1)} %wq_in.1, bf16[4096,128]{1,0:T(8,128)(2,1)} %wk_in.1, bf16[4096,128]{1,0:T(8,128)(2,1)} %wv_in.1, s32[128]{0:T(128)} %blocks.1, f32[2,128,128]{2,1,0:T(8,128)} %constant.4.clone.base, f32[2,128,128]{2,1,0:T(8,128)} %constant.5.clone.offset), custom_call_target="tpu_custom_call" | custom-call | flops 38000001024 | bytes 12000000 | tf_op jit(solution)/shard_map/pallas_call | solution.py:502
  74.4 1.9 %copy.9 = bf16[256,1024]{1,0:T(8,128)(2,1)} copy(bf16[256,1024]{1,0:T(8,128)(2,1)} %shard_map.73) | data formatting | bytes 1048576

commit v5 on v4

--- a/solution.py
+++ b/solution.py
@@ -460,8 +460,7 @@
                 communicate(step_acts[low])
             else:
                 middle = (low + high) // 2
-                pl.when(step < middle)(lambda: pick(low, middle))
-                pl.when(step >= middle)(lambda: pick(middle, high))
+                lax.cond(step < middle, lambda: pick(low, middle), lambda: pick(middle, high))
 
         pick(0, len(step_acts))
         attend([(1, step), (0, step + AHEAD)])

time: 76.4 us -> 76.4 us (level)
  no operation moved by 1% of the time
where the time goes in v5:
time: 76.4 us; the launch traced here: 76.3 us
  Pallas kernels  74.4 us (97%)
  local copies, waits for them, and re-layouts  1.87 us (2%)
    pallas_call x1, Pallas kernels, per_device(): pl.pallas_call(kernel, out_shape=jax.ShapeDtypeStruct((256, 1024), jnp.bf...  74.4 us
    unnamed x1, local copies, waits for them, and re-layouts  1.87 us

profile of v5, /device:TPU:1, one launch (start us, length us, event | category | flops | bytes accessed | tf_op | source)
XLA Modules:
  0.0 76.3 jit_solution(1492250750124152870)
XLA Ops:
  0.0 74.4 %shard_map.73 = bf16[256,1024]{1,0:T(8,128)(2,1)} custom-call(bf16[64,4096]{1,0:T(8,128)(2,1)} %tok_in.1, bf16[4096,1024]{1,0:T(8,128)(2,1)} %wq_in.1, bf16[4096,128]{1,0:T(8,128)(2,1)} %wk_in.1, bf16[4096,128]{1,0:T(8,128)(2,1)} %wv_in.1, s32[128]{0:T(128)} %blocks.1, f32[2,128,128]{2,1,0:T(8,128)} %constant.4.clone.base, f32[2,128,128]{2,1,0:T(8,128)} %constant.5.clone.offset), custom_call_target="tpu_custom_call" | custom-call | flops 38000001024 | bytes 12000000 | tf_op jit(solution)/shard_map/pallas_call | solution.py:501
  74.4 1.9 %copy.9 = bf16[256,1024]{1,0:T(8,128)(2,1)} copy(bf16[256,1024]{1,0:T(8,128)(2,1)} %shard_map.73) | data formatting | bytes 1048576

commit v6 on v5

--- a/solution.py
+++ b/solution.py
@@ -14,7 +14,7 @@
 CHUNKS = 16
 ROWS = 1024
 HALF = 64
-TILE = 512
+TILE = 1024
 WIDE = 256
 AHEAD = 0
 LOW = -1e30

time: 76.4 us -> 76.3 us (level)
  no operation moved by 1% of the time
where the time goes in v6:
time: 76.3 us; the launch traced here: 76.1 us
  Pallas kernels  74.3 us (97%)
  local copies, waits for them, and re-layouts  1.87 us (2%)
    pallas_call x1, Pallas kernels, per_device(): pl.pallas_call(kernel, out_shape=jax.ShapeDtypeStruct((256, 1024), jnp.bf...  74.3 us
    unnamed x1, local copies, waits for them, and re-layouts  1.87 us

profile of v6, /device:TPU:1, one launch (start us, length us, event | category | flops | bytes accessed | tf_op | source)
XLA Modules:
  0.0 76.1 jit_solution(8252734585671577008)
XLA Ops:
  0.0 74.3 %shard_map.73 = bf16[256,1024]{1,0:T(8,128)(2,1)} custom-call(bf16[64,4096]{1,0:T(8,128)(2,1)} %tok_in.1, bf16[4096,1024]{1,0:T(8,128)(2,1)} %wq_in.1, bf16[4096,128]{1,0:T(8,128)(2,1)} %wk_in.1, bf16[4096,128]{1,0:T(8,128)(2,1)} %wv_in.1, s32[128]{0:T(128)} %blocks.1, f32[2,128,128]{2,1,0:T(8,128)} %constant.4.clone.base, f32[2,128,128]{2,1,0:T(8,128)} %constant.5.clone.offset), custom_call_target="tpu_custom_call" | custom-call | flops 38000001024 | bytes 12000000 | tf_op jit(solution)/shard_map/pallas_call | solution.py:501
  74.3 1.9 %copy.9 = bf16[256,1024]{1,0:T(8,128)(2,1)} copy(bf16[256,1024]{1,0:T(8,128)(2,1)} %shard_map.73) | data formatting | bytes 1048576
